TPU v7x, 32 devices: a whole 2x2x4 slice. The times are simulated.
32 devices in a mesh: parts: 2 (over x), types: 8 (over z, y), tm: 2 (over core).
Axes of the slice: x: 2, y: 2, z: 4, core: 2. Of those that a mesh axis runs over, the one named last changes fastest.
Arguments:
- counts: int32 [1024, 8192], P(('parts', 'tm'), 'types'), parts along dimension 0, may hold values from 0 to 3
- mark_value: bfloat16 [1024, 8192], P(('parts', 'tm'), 'types'), parts along dimension 0, may hold values from 0.25 to 4
- base_rate: float32 [8192], P('types'), may hold values from 0.2 to 2
- excite: bfloat16 [4, 64, 6, 128, 128], P(None, 'types'), may hold values from -0.109375 to 0.109375
- block_col: int32 [64, 6], replicated, may hold values from 0 to 63, as said below
- row_fill: int32 [64], replicated, may hold values from 2 to 6, as said below
Outputs:
- grad_excite: bfloat16 [8, 64, 6, 128, 128], P('parts', 'types', None, 'tm'), parts along dimension 0
- grad_rate: float32 [16384], P(('parts', 'types', 'tm')), parts along dimension 0
There are 2 independent parts, one for each index of `parts`. A program takes and returns all parts, laid end to end along the dimension named above; an argument that names none is the same for every part. Nothing has to cross between parts.
Inputs may be any that keep to these rules, and one draw needn't show every extreme that they name: `block_col`: among the live blocks of the 8 block rows of one device, at most 6 name column blocks held by any one device (column block c is held by device c // 8); every device has exactly 6 such blocks from some device in every draw. `row_fill`: the first of each device's 8 block rows has all 6 blocks live.
All inputs are finite; a program needn't handle non-finite values.
Results may differ from a plain program's by a relative error of at most 0.012.
Values may be sent and summed in bfloat16 or wider, within the bound.
No kernel may reach another device: no remote copies, remote signals or barrier semaphores. Data moves between devices by JAX's collectives and lax.ppermute only.
A program may use at most 128 MiB of HBM per device.

v0:
```python
import functools
import jax
import jax.numpy as jnp
from jax import lax
from jax.experimental import pallas as pl
from jax.experimental.pallas import tpu as pltpu
from jax.sharding import PartitionSpec as P

GROUPS = 2
SMEM = pl.BlockSpec(memory_space=pltpu.SMEM)
VMEM = pl.BlockSpec(memory_space=pltpu.VMEM)
ANYWHERE = pl.BlockSpec(memory_space=pl.ANY)
PARAMS = pltpu.CompilerParams(vmem_limit_bytes=16 << 20)


def lag_tables(bins, basis_count, overall, lanes):
    log_decay = -(8.0 ** jnp.arange(basis_count, dtype=jnp.float32)) / (2.0 * overall)
    t = jnp.arange(bins, dtype=jnp.float32)
    lag = t[:, None] - 1.0 - t[None, :]
    weights = jnp.where(
        lag[None] >= 0.0,
        (1.0 - jnp.exp(log_decay))[:, None, None]
        * jnp.exp(jnp.maximum(lag, 0.0)[None] * log_decay[:, None, None]),
        jnp.float32(0.0),
    )
    power = jnp.exp(t[None, :, None] * log_decay[:, None, None])
    return weights.astype(jnp.bfloat16), jnp.broadcast_to(power, (basis_count, bins, lanes))


def load_lanes(first, count, parts, counts_hbm, mark_hbm, counts, mark, sems):
    lanes = count // parts
    copies = []
    for j in range(parts):
        at = pl.ds(first + j * lanes, lanes)
        to = pl.ds(j * lanes, lanes)
        copies.append(
            (
                pltpu.make_async_copy(counts_hbm.at[:, at], counts.at[:, to], sems.at[0, j]),
                pltpu.make_async_copy(mark_hbm.at[:, at], mark.at[:, to], sems.at[1, j]),
            )
        )
        for copy in copies[-1]:
            copy.start()
    return copies


def impact_of(counts, mark, at):
    impact = counts[:, at].astype(jnp.float32) * mark[:, at].astype(jnp.float32)
    return impact.astype(jnp.bfloat16)


def first_kernel(counts_hbm, mark_hbm, out_ref, counts, mark, sems):
    bins, lanes = counts.shape
    tile = out_ref.shape[1]
    parts = sems.shape[1]
    copies = load_lanes(0, lanes, parts, counts_hbm, mark_hbm, counts, mark, sems)
    for j in range(parts):
        for copy in copies[j]:
            copy.wait()
        for q in range(j * lanes // parts // tile, (j + 1) * lanes // parts // tile):
            at = slice(q * tile, (q + 1) * tile)
            out_ref[q * bins : (q + 1) * bins] = impact_of(counts, mark, at)


def second_kernel(
    basis, tile, overall, counts_hbm, mark_hbm, out_ref, ends_ref, counts, mark, sems
):
    bins, types = counts.shape
    parts = sems.shape[1]
    lanes = types // parts
    copies = load_lanes(0, types, parts, counts_hbm, mark_hbm, counts, mark, sems)
    back = (bins - 1 - lax.broadcasted_iota(jnp.int32, (bins, tile), 0)).astype(jnp.float32)
    gains = []
    for b in range(basis):
        rate = (8.0**b) / (2.0 * overall)
        gains.append((1.0 - jnp.exp(jnp.full((bins, tile), -rate, jnp.float32))) * jnp.exp(-rate * back))
    half = types // tile // 2
    for j in range(parts):
        for copy in copies[j]:
            copy.wait()
        for block in range(j * lanes // tile, (j + 1) * lanes // tile):
            at = slice(block * tile, (block + 1) * tile)
            impact = impact_of(counts, mark, at)
            if block >= half:
                out_ref[(block - half) * bins : (block - half + 1) * bins] = impact
            impact = impact.astype(jnp.float32)
            for b in range(basis):
                ends_ref[b : b + 1, at] = jnp.sum(impact * gains[b], axis=0, keepdims=True)
    rest = out_ref.shape[0] - half * bins
    out_ref[half * bins :] = jnp.zeros((rest, tile), jnp.bfloat16)


def carry_rows(half, basis):
    return -(-half * basis // 16) * 16


def impact_messages(counts, mark, dims, overall):
    basis, _, _, tile = dims
    bins, types = counts.shape
    half = types // tile // 2
    params = pltpu.CompilerParams(vmem_limit_bytes=56 << 20)
    one = pl.pallas_call(
        first_kernel,
        in_specs=[ANYWHERE, ANYWHERE],
        out_specs=VMEM,
        out_shape=jax.ShapeDtypeStruct((half * bins, tile), jnp.bfloat16),
        scratch_shapes=[
            pltpu.VMEM((bins, types // 2), jnp.int32),
            pltpu.VMEM((bins, types // 2), jnp.bfloat16),
            pltpu.SemaphoreType.DMA((2, 2)),
        ],
        compiler_params=params,
        name="first_message",
    )(counts, mark)
    two, ends = pl.pallas_call(
        functools.partial(second_kernel, basis, tile, overall),
        in_specs=[ANYWHERE, ANYWHERE],
        out_specs=[VMEM, VMEM],
        out_shape=[
            jax.ShapeDtypeStruct((half * bins + 2 * carry_rows(half, basis), tile), jnp.bfloat16),
            jax.ShapeDtypeStruct((basis, types), jnp.float32),
        ],
        scratch_shapes=[
            pltpu.VMEM((bins, types), jnp.int32),
            pltpu.VMEM((bins, types), jnp.bfloat16),
            pltpu.SemaphoreType.DMA((2, 2)),
        ],
        compiler_params=params,
        name="second_message",
    )(counts, mark)
    return one, two, ends


def carry_kernel(basis, bins, enter_ref, _, out_ref, held, sem):
    rows, tile = out_ref.shape
    half = enter_ref.shape[1] // tile // 2
    each = carry_rows(half, basis)
    carry = []
    for d in range(2):
        for q in range(half):
            carry.append(enter_ref[:, (d * half + q) * tile : (d * half + q + 1) * tile])
        if each > half * basis:
            carry.append(jnp.zeros((each - half * basis, tile), jnp.float32))
    held[...] = jnp.concatenate(carry, axis=0).astype(jnp.bfloat16)
    copy = pltpu.make_async_copy(held, out_ref.at[pl.ds(half * bins, 2 * each)], sem)
    copy.start()
    copy.wait()


def add_carry(enter, two, basis, bins):
    rows, tile = two.shape
    return pl.pallas_call(
        functools.partial(carry_kernel, basis, bins),
        in_specs=[VMEM, ANYWHERE],
        out_specs=ANYWHERE,
        out_shape=jax.ShapeDtypeStruct(two.shape, two.dtype),
        scratch_shapes=[
            pltpu.VMEM((rows % bins, tile), jnp.bfloat16),
            pltpu.SemaphoreType.DMA,
        ],
        input_output_aliases={1: 0},
        compiler_params=PARAMS,
        name="carry_rows",
    )(enter, two)


def ring_place(index, n):
    return jnp.where((index & 1) == 0, index >> 1, n - 1 - (index >> 1))


def code_of(row, slot, block):
    return (row * 256 + slot) * 256 + block


def plan_kernel(shape, col_ref, fill_ref, plan_ref):
    brows, slots, width, n, most = shape
    own = lax.axis_index("types")
    calls = n // 2 + 1
    tail = calls * (most + 1)
    plan_ref[tail] = lax.axis_index("tm")
    for step in range(calls):
        plan_ref[step * (most + 1)] = 0

    @pl.loop(0, brows)
    def _(row):
        fill = fill_ref[own * brows + row]
        plan_ref[tail + 1 + row] = fill

        @pl.loop(0, fill)
        def _(slot):
            column = col_ref[own * brows + row, slot]
            shift = width.bit_length() - 1
            even = width == 1 << shift
            source = column >> shift if even else lax.div(column, width)
            block = column & (width - 1) if even else lax.rem(column, width)
            ahead = ring_place(source, n) - ring_place(own, n)
            ahead = jnp.where(ahead < 0, ahead + n, ahead)
            call = jnp.minimum(ahead, n - ahead)
            down = (ahead > 0) & (ahead < n // 2)
            base = call * (most + 1)
            count = plan_ref[base] + 1
            plan_ref[base] = count
            plan_ref[base + count] = code_of(row, slot, jnp.where(down, width + block, block))

    for step in range(calls):
        base = step * (most + 1)
        count = plan_ref[base]

        @pl.when(lax.rem(count, 2) == 1)
        def _(base=base, count=count):
            plan_ref[base + count + 1] = code_of(brows, 0, 0)


def make_plan(cols, fill, dims, width, n):
    _, brows, slots, _ = dims
    most = 2 * max(2, brows * slots // n)
    return pl.pallas_call(
        functools.partial(plan_kernel, (brows, slots, width, n, most)),
        in_specs=[SMEM] * 2,
        out_specs=SMEM,
        out_shape=jax.ShapeDtypeStruct(((n // 2 + 1) * (most + 1) + 1 + brows,), jnp.int32),
        compiler_params=PARAMS,
        name="plan",
    )(cols, fill)


def start_kernel(tile, counts_ref, base_ref, total_ref):
    for row in range(total_ref.shape[0] - 1):
        at = slice(row * tile, (row + 1) * tile)
        total_ref[row] = base_ref[:, at] - counts_ref[:, at].astype(jnp.float32)
    total_ref[total_ref.shape[0] - 1] = jnp.zeros(total_ref.shape[1:], jnp.float32)


def start_total(counts, base_rate, dims):
    _, brows, _, tile = dims
    return pl.pallas_call(
        functools.partial(start_kernel, tile),
        in_specs=[VMEM, VMEM],
        out_specs=VMEM,
        out_shape=jax.ShapeDtypeStruct((brows + 1, counts.shape[0], tile), jnp.float32),
        compiler_params=PARAMS,
        name="base_less_counts",
    )(counts, base_rate)


def step_kernel(dims, n, call, groups, plan_ref, *refs):
    basis, brows, slots, tile = dims
    lag_ref, power_ref, excite_ref = refs[len(groups) : len(groups) + 3]
    total_in, states_ref, total_ref, built_ref, held, weights, sems = refs[-7:]
    bins = lag_ref.shape[1]
    half = held.shape[0] // len(groups)
    each = carry_rows(half, basis)
    most = (plan_ref.shape[0] - 1 - brows) // (n // 2 + 1) - 1
    built_ref[...] = jnp.zeros_like(built_ref)
    pairs = (plan_ref[call * (most + 1)] + 1) // 2

    def entry_at(place):
        code = plan_ref[call * (most + 1) + 1 + place]
        return code >> 16, (code >> 8) & 255, code & 255

    def weight_at(place):
        row, slot, _ = entry_at(place)
        return pltpu.make_async_copy(
            excite_ref.at[:, jnp.minimum(row, brows - 1), slot],
            weights.at[place],
            sems.at[0, place],
        )

    def copy_at(place):
        row, slot, block = entry_at(place)
        return pltpu.make_async_copy(
            held.at[block], states_ref.at[row * slots + slot], sems.at[1, place]
        )

    @pl.loop(0, 2 * pairs)
    def _(place):
        weight_at(place).start()

    total_ref[...] = total_in[...]
    for d, (carried_by, second) in enumerate(groups):
        impact_ref, carry_ref = refs[d], refs[carried_by]
        first = half * bins + second * each
        carry = carry_ref[first : first + each].astype(jnp.float32)
        for q in range(0, half, 2):
            both = jnp.concatenate(
                [impact_ref[(q + i) * bins : (q + i + 1) * bins] for i in range(2)], axis=1
            )
            for b in range(basis):
                state = jnp.dot(lag_ref[b], both, preferred_element_type=jnp.float32)
                for i in range(2):
                    row = (q + i) * basis + b
                    held[d * half + q + i, :, b * tile : (b + 1) * tile] = (
                        state[:, i * tile : (i + 1) * tile] + power_ref[b] * carry[row : row + 1]
                    ).astype(jnp.bfloat16)

    @pl.loop(0, 2 * pairs)
    def _(place):
        copy_at(place).start()

    @pl.loop(0, pairs)
    def _(k):
        terms = []
        for i in range(2):
            row, _, block = entry_at(2 * k + i)
            weight_at(2 * k + i).wait()
            weight = jnp.concatenate([weights[2 * k + i, b] for b in range(basis)], axis=1)
            term = lax.dot_general(
                held[block], weight, (((1,), (1,)), ((), ())), preferred_element_type=jnp.float32
            )
            terms.append((row, term))
        for row, term in terms:
            total_ref[row] += term

    @pl.loop(0, 2 * pairs)
    def _(place):
        copy_at(place).wait()


def take_step(call, groups, plan, arrived, lag, power, excite, states, total, dims, n):
    basis, brows, slots, tile = dims
    bins = lag.shape[1]
    half = arrived[0].shape[0] // bins
    most = (plan.shape[0] - 1 - brows) // (n // 2 + 1) - 1
    given = [total] if states is None else [states, total]
    return pl.pallas_call(
        functools.partial(step_kernel, dims, n, call, groups),
        in_specs=[SMEM] + [VMEM] * (len(groups) + 2) + [ANYWHERE] * len(given) + [VMEM],
        out_specs=[ANYWHERE, VMEM, VMEM],
        out_shape=[
            jax.ShapeDtypeStruct((brows * slots + 1, bins, basis * tile), jnp.bfloat16),
            jax.ShapeDtypeStruct(total.shape, total.dtype),
            jax.ShapeDtypeStruct((8, tile), jnp.float32),
        ],
        scratch_shapes=[
            pltpu.VMEM((len(groups) * half, bins, basis * tile), jnp.bfloat16),
            pltpu.VMEM((most, basis, tile, tile), jnp.bfloat16),
            pltpu.SemaphoreType.DMA((2, most)),
        ],
        input_output_aliases={} if states is None else {len(groups) + 4: 0},
        compiler_params=PARAMS,
        cost_estimate=pl.CostEstimate(
            flops=8 * basis * bins * bins * tile * 4,
            bytes_accessed=4 * 1024 * 1024,
            transcendentals=0,
        ),
        name="ring_step",
    )(plan, *arrived, lag, power, excite, *given)


def products(turned_ref, states_ref, plan_ref, group, dims, sent_ref, kept_ref):
    basis, brows, slots, tile = dims
    tail = plan_ref.shape[0] - 1 - brows
    part = tile // 2
    for r, row in enumerate(rows_of(group, dims)):
        fill = plan_ref[tail + 1 + row]
        for s in range(slots):
            grad = jnp.dot(
                turned_ref[row], states_ref[row * slots + s], preferred_element_type=jnp.float32
            )
            grad = jnp.where(s < fill, grad, jnp.zeros_like(grad))
            for b in range(basis):
                at = slice(b * tile, (b + 1) * tile)
                kept_ref[b, r, s] = grad[:part, at]
                sent_ref[b, r, s] = grad[part:, at].astype(sent_ref.dtype)


def rows_of(group, dims):
    count = dims[1] // GROUPS
    return range(group * count, (group + 1) * count)


def weighted_kernel(dims, overall, plan_ref, total_ref, states_ref, sent_ref, kept_ref, *refs):
    _, brows, _, tile = dims
    turned_ref, rate_sent_ref, rate_kept_ref = refs
    half = plan_ref[plan_ref.shape[0] - 1 - brows]
    part = tile // 2
    rates = []
    for row in range(brows):
        weighted = (2.0 / overall) * total_ref[row]
        rates.append(jnp.sum(weighted, axis=0, keepdims=True))
        weighted = weighted.T.astype(jnp.bfloat16)
        upper, lower = weighted[:part], weighted[part:]
        turned_ref[row, :part] = jnp.where(half == 0, upper, lower)
        turned_ref[row, part:] = jnp.where(half == 0, lower, upper)
    first_half = jnp.concatenate(rates[: brows // 2], axis=0)
    second_half = jnp.concatenate(rates[brows // 2 :], axis=0)
    rate_kept_ref[...] = jnp.where(half == 0, first_half, second_half)
    rate_sent_ref[...] = jnp.where(half == 0, second_half, first_half)
    products(turned_ref, states_ref, plan_ref, 0, dims, sent_ref, kept_ref)


def later_kernel(dims, group, plan_ref, turned_ref, states_ref, sent_ref, kept_ref):
    products(turned_ref, states_ref, plan_ref, group, dims, sent_ref, kept_ref)


def group_shape(dims, dtype):
    basis, brows, slots, tile = dims
    return jax.ShapeDtypeStruct((basis, brows // GROUPS, slots, tile // 2, tile), dtype)


def first_products(plan, total, states, dims, overall):
    _, brows, _, tile = dims
    turned = jax.ShapeDtypeStruct((brows, tile, total.shape[1]), jnp.bfloat16)
    rate = jax.ShapeDtypeStruct((brows // 2, tile), jnp.float32)
    return pl.pallas_call(
        functools.partial(weighted_kernel, dims, overall),
        in_specs=[SMEM, VMEM, VMEM],
        out_specs=[VMEM] * 5,
        out_shape=[
            group_shape(dims, jnp.bfloat16),
            group_shape(dims, jnp.float32),
            turned,
            rate,
            rate,
        ],
        compiler_params=PARAMS,
        name="weighted_products",
    )(plan, total, states)


def later_products(group, plan, turned, states, dims):
    return pl.pallas_call(
        functools.partial(later_kernel, dims, group),
        in_specs=[SMEM, VMEM, VMEM],
        out_specs=[VMEM, VMEM],
        out_shape=[group_shape(dims, jnp.bfloat16), group_shape(dims, jnp.float32)],
        compiler_params=PARAMS,
        name="products",
    )(plan, turned, states)


def add_kernel(dims, group, kept_ref, got_ref, *refs):
    basis, brows, _, _ = dims
    out_ref, held, sems = refs[-3:]
    if group == GROUPS - 1:
        rate_ref, rate_got_ref, rate_out_ref = refs[0], refs[1], refs[-4]
        out_ref, rate_out_ref = rate_out_ref, out_ref
        rate_out_ref[...] = rate_ref[...] + rate_got_ref[...]
    copies = []
    for r, row in enumerate(rows_of(group, dims)):
        for b in range(basis):
            held[b, r] = (kept_ref[b, r] + got_ref[b, r].astype(jnp.float32)).astype(jnp.bfloat16)
            copies.append(
                pltpu.make_async_copy(held.at[b, r], out_ref.at[b, row], sems.at[b, r])
            )
            copies[-1].start()
    for copy in copies:
        copy.wait()


def add_received(group, kept, got, rates, grad, dims):
    basis, brows, slots, tile = dims
    whole = jax.ShapeDtypeStruct((basis, brows, slots, tile // 2, tile), jnp.bfloat16)
    given = [] if grad is None else [grad]
    last = group == GROUPS - 1
    return pl.pallas_call(
        functools.partial(add_kernel, dims, group),
        in_specs=[VMEM] * (2 + len(rates)) + [ANYWHERE] * len(given),
        out_specs=[ANYWHERE, VMEM] if last else [ANYWHERE],
        out_shape=[whole] + ([jax.ShapeDtypeStruct(rates[0].shape, jnp.float32)] if last else []),
        scratch_shapes=[
            pltpu.VMEM(group_shape(dims, jnp.bfloat16).shape, jnp.bfloat16),
            pltpu.SemaphoreType.DMA((basis, brows // GROUPS)),
        ],
        input_output_aliases={2 + len(rates): 0} if given else {},
        compiler_params=PARAMS,
        name="add_received",
    )(kept, got, *rates, *given)


def shards(counts, mark_value, base_rate, excite, block_col, row_fill):
    dims = excite.shape[:4]
    basis, _, _, tile = dims
    bins = counts.shape[0]
    overall = bins * lax.axis_size("tm")
    n = lax.axis_size("types")
    order = list(range(0, n, 2)) + list(range(1, n, 2))[::-1]
    up = [(order[i], order[(i + 1) % n]) for i in range(n)]
    down = [(b, a) for a, b in up]
    swap = [(0, 1), (1, 0)]

    one, two, ends = impact_messages(counts, mark_value, dims, overall)
    enter = lax.ppermute(ends, "tm", [(0, 1)])
    two = add_carry(enter, two, basis, bins)
    lag, power = lag_tables(bins, basis, overall, tile)

    states = None
    built = []

    def after(value, message):
        return lax.optimization_barrier((value, message))[0]

    def step(groups, arrived):
        nonlocal states, total
        states, total, done = take_step(
            len(built), groups, plan, arrived, lag, power, excite, states, total, dims, n
        )
        built.append(done)

    def send(message, way, hop):
        if hop > 2:
            message = after(message, built[hop - 3])
        return lax.ppermute(message, "types", way)

    two_groups = ((1, 0), (1, 1))
    hops = n // 2
    at_up, at_down = [one, two], [one, two]
    for hop in range(1, hops + 1):
        if 1 < hop < hops:
            ready = (at_up[0], at_down[0]) + ((plan,) if hop == 2 else ())
            at_up = [at_up[0], after(at_up[1], ready)]
            at_down = [at_down[0], after(at_down[1], ready)]
        if hop < hops:
            next_up, next_down = [None, None], [None, None]
            for second in range(2):
                next_up[second] = send(at_up[second], up, hop)
                next_down[second] = send(at_down[second], down, hop)
        else:
            next_up = [send(at_up[0], up, hop), None]
            next_down = [None, send(at_down[1], down, hop)]
        if hop == 1:
            cols = after(block_col, (next_up[0], next_down[0]))
            plan = make_plan(cols, row_fill, dims, counts.shape[1] // tile, n)
            total = start_total(counts, base_rate.reshape(1, -1), dims)
            total = after(total, next_up[1])
            step(two_groups, [one, two])
        else:
            step(((1, 0), (1, 1), (3, 0), (3, 1)), [*at_up, *at_down])
        at_up, at_down = next_up, next_down
    step(two_groups, [at_up[0], at_down[1]])

    out, kept, turned, rate_sent, rate_kept = first_products(plan, total, states, dims, overall)
    kept = [kept]
    got = [lax.ppermute(out, "tm", swap)]
    rate_got = lax.ppermute(rate_sent, "tm", swap)
    for group in range(1, GROUPS):
        out, more = later_products(group, plan, turned, states, dims)
        kept.append(more)
        got.append(lax.ppermute(out, "tm", swap))
    grad = None
    for group in range(GROUPS):
        rates = [rate_kept, rate_got] if group == GROUPS - 1 else []
        grad, *rate = add_received(group, kept[group], got[group], rates, grad, dims)
    return grad, rate[0].reshape(-1)


def solution(mesh):
    return jax.shard_map(
        shards,
        mesh=mesh,
        in_specs=(
            P(("parts", "tm"), "types"),
            P(("parts", "tm"), "types"),
            P("types"),
            P(None, "types", None, None, None),
            P(),
            P(),
        ),
        out_specs=(P("parts", "types", None, "tm", None), P(("parts", "types", "tm"))),
        check_vma=False,
    )
```

profile of v0, /device:TPU:0, one launch (start us, length us, event | category | flops | bytes accessed | tf_op | source)
XLA Modules:
  0.0 69.5 jit_solution(14377860946868672046)
XLA Ops:
  0.7 2.0 %first_message.1.refs_0_ = bf16[1024,128]{1,0:T(8,128)(2,1)} custom-call(s32[256,1024]{1,0:T(8,128)} %counts_ref.1, bf16[256,1024]{1,0:T(8,128)(2,1)} %mark_hbm.3), custom_call_target="tpu_custom_call" | custom-call | tf_op jit(solution)/shard_map/first_message/pallas_call | solution.py:102
  2.7 3.1 %collective-permute-start = (bf16[1024,128]{1,0:T(8,128)(2,1)}, bf16[1024,128]{1,0:T(8,128)(2,1)S(1)}, u32[]{:S(2)}, u32[]{:S(2)}) collective-permute-start(bf16[1024,128]{1,0:T(8,128)(2,1)} %first_message.1.refs_0_), channel_id=1, source_target_pairs={{0,4},{4,8},{8,12},{12,14},{14,10},{10,6},{6,2},{2,0},{1,5},{5,9},... | collective-permute-start | bytes 786440 | tf_op jit(solution)/shard_map/ppermute | solution.py:503
  5.8 2.5 %second_message.1 = (bf16[1056,128]{1,0:T(8,128)(2,1)}, f32[4,1024]{1,0:T(4,128)}) custom-call(s32[256,1024]{1,0:T(8,128)} %counts_ref.1, bf16[256,1024]{1,0:T(8,128)(2,1)} %mark_hbm.3), custom_call_target="tpu_custom_call" | custom-call | tf_op jit(solution)/shard_map/second_message/pallas_call | solution.py:115
  8.2 1.5 %collective-permute-start.3 = (f32[4,1024]{1,0:T(4,128)}, f32[4,1024]{1,0:T(4,128)S(1)}, u32[]{:S(2)}, u32[]{:S(2)}) collective-permute-start(f32[4,1024]{1,0:T(4,128)} %get-tuple-element.38), channel_id=1, source_target_pairs={{0,1},{2,3},{4,5},{6,7},{8,9},{10,11},{12,13},{14,15},{16,17},{18,... | collective-permute-start | bytes 49160 | tf_op jit(solution)/shard_map/ppermute | solution.py:483
  11.3 1.8 %collective-permute-start.6 = (bf16[1056,128]{1,0:T(8,128)(2,1)}, bf16[1056,128]{1,0:T(8,128)(2,1)S(1)}, u32[]{:S(2)}, u32[]{:S(2)}) collective-permute-start(bf16[1056,128]{1,0:T(8,128)(2,1)} %carry_rows.1.refs_1_), channel_id=1, source_target_pairs={{4,0},{8,4},{12,8},{14,12},{10,14},{6,10},{2,6},{0,2},{5,1},{9,5},... | collective-permute-start | bytes 811016 | tf_op jit(solution)/shard_map/ppermute | solution.py:503
  14.0 2.5 %plan.1.plan_ref = s32[74]{0:T(128)S(1)} custom-call(s32[64,6]{1,0:T(8,128)S(1)} %copy.14.col_ref, s32[64]{0:T(128)S(1)} %copy-done.4), custom_call_target="tpu_custom_call" | custom-call | tf_op jit(solution)/shard_map/plan/pallas_call | solution.py:217
  16.5 1.8 %collective-permute-start.2 = (bf16[1024,128]{1,0:T(8,128)(2,1)S(1)}, bf16[1024,128]{1,0:T(8,128)(2,1)S(1)}, u32[]{:S(2)}, u32[]{:S(2)}) collective-permute-start(bf16[1024,128]{1,0:T(8,128)(2,1)S(1)} %collective-permute-done.refs_0_), channel_id=1, source_target_pairs={{0,4},{4,8},{8,12},{12,14},{14,10},{10,6},{6,2},{2,0},{1,5},{5,9},... | collective-permute-start | bytes 786440 | tf_op jit(solution)/shard_map/ppermute | solution.py:503
  18.6 1.9 %collective-permute-done.6.refs_3_ = bf16[1056,128]{1,0:T(8,128)(2,1)S(1)} collective-permute-done((bf16[1056,128]{1,0:T(8,128)(2,1)}, bf16[1056,128]{1,0:T(8,128)(2,1)S(1)}, u32[]{:S(2)}, u32[]{:S(2)}) %collective-permute-start.6) | collective-permute-done | bytes 270368 | tf_op jit(solution)/shard_map/ppermute | solution.py:503
  20.4 2.2 %collective-permute-start.8 = (bf16[1056,128]{1,0:T(8,128)(2,1)S(1)}, bf16[1056,128]{1,0:T(8,128)(2,1)S(1)}, u32[]{:S(2)}, u32[]{:S(2)}) collective-permute-start(bf16[1056,128]{1,0:T(8,128)(2,1)S(1)} %collective-permute-done.6.refs_3_), channel_id=1, source_target_pairs={{4,0},{8,4},{12,8},{14,12},{10,14},{6,10},{2,6},{0,2},{5,1},{9,5},... | collective-permute-start | bytes 811016 | tf_op jit(solution)/shard_map/ppermute | solution.py:503
  23.2 2.8 %copy-done = bf16[4,8,6,128,128]{4,3,2,1,0:T(8,128)(2,1)S(1)} copy-done((bf16[4,8,6,128,128]{4,3,2,1,0:T(8,128)(2,1)S(1)}, bf16[4,8,6,128,128]{4,3,2,1,0:T(8,128)(2,1)}, u32[]{:S(2)}) %copy-start) | copy-done | bytes 6291480
  26.0 4.5 %ring_step.5 = (bf16[49,256,512]{2,1,0:T(8,128)(2,1)S(1)}, f32[9,256,128]{2,1,0:T(8,128)S(1)}, f32[8,128]{1,0:T(8,128)}) custom-call(s32[74]{0:T(128)S(1)} %plan.1.plan_ref, bf16[1024,128]{1,0:T(8,128)(2,1)S(1)} %copy-done.2, bf16[1056,128]{1,0:T(8,128)(2,1)} %carry_rows.1.refs_1_, bf16[4,256,256]{2,1,0:T(8,128)(2,1)S(1)} %select_convert_fusion.refs_2_.refs_4_, ...), custom_call_target="tpu_custom_call" | custom-call | flops 1073741824 | bytes 4194304 | tf_op jit(solution)/shard_map/ring_step/pallas_call | solution.py:325
  30.5 1.3 %collective-permute-done.8.refs_3_ = bf16[1056,128]{1,0:T(8,128)(2,1)S(1)} collective-permute-done((bf16[1056,128]{1,0:T(8,128)(2,1)S(1)}, bf16[1056,128]{1,0:T(8,128)(2,1)S(1)}, u32[]{:S(2)}, u32[]{:S(2)}) %collective-permute-start.8) | collective-permute-done | bytes 270368 | tf_op jit(solution)/shard_map/ppermute | solution.py:503
  31.9 1.7 %collective-permute-start.10 = (bf16[1056,128]{1,0:T(8,128)(2,1)S(1)}, bf16[1056,128]{1,0:T(8,128)(2,1)S(1)}, u32[]{:S(2)}, u32[]{:S(2)}) collective-permute-start(bf16[1056,128]{1,0:T(8,128)(2,1)S(1)} %collective-permute-done.8.refs_3_), channel_id=1, source_target_pairs={{4,0},{8,4},{12,8},{14,12},{10,14},{6,10},{2,6},{0,2},{5,1},{9,5},... | collective-permute-start | bytes 811016 | tf_op jit(solution)/shard_map/ppermute | solution.py:503
  33.9 1.7 %collective-permute-start.14 = (bf16[1024,128]{1,0:T(8,128)(2,1)S(1)}, bf16[1024,128]{1,0:T(8,128)(2,1)S(1)}, u32[]{:S(2)}, u32[]{:S(2)}) collective-permute-start(bf16[1024,128]{1,0:T(8,128)(2,1)S(1)} %collective-permute-done.9.refs_2_), channel_id=1, source_target_pairs={{4,0},{8,4},{12,8},{14,12},{10,14},{6,10},{2,6},{0,2},{5,1},{9,5},... | collective-permute-start | bytes 786440 | tf_op jit(solution)/shard_map/ppermute | solution.py:503
  35.9 5.3 %ring_step.6 = (bf16[49,256,512]{2,1,0:T(8,128)(2,1)S(1)}, f32[9,256,128]{2,1,0:T(8,128)S(1)}, f32[8,128]{1,0:T(8,128)}) custom-call(s32[74]{0:T(128)S(1)} %plan.1.plan_ref, bf16[1024,128]{1,0:T(8,128)(2,1)S(1)} %collective-permute-done.refs_0_, bf16[1056,128]{1,0:T(8,128)(2,1)S(1)} %collective-permute-done.4.refs_1_, ...), custom_call_target="tpu_custom_call", output_to_operand_aliasing={{0}: (8, {})} | custom-call | flops 1073741824 | bytes 4194304 | tf_op jit(solution)/shard_map/ring_step/pallas_call | solution.py:325
  41.3 1.7 %collective-permute-start.11 = (bf16[1056,128]{1,0:T(8,128)(2,1)S(1)}, bf16[1056,128]{1,0:T(8,128)(2,1)S(1)}, u32[]{:S(2)}, u32[]{:S(2)}) collective-permute-start(bf16[1056,128]{1,0:T(8,128)(2,1)S(1)} %collective-permute-done.10.refs_3_), channel_id=1, source_target_pairs={{4,0},{8,4},{12,8},{14,12},{10,14},{6,10},{2,6},{0,2},{5,1},{9,5},... | collective-permute-start | bytes 811016 | tf_op jit(solution)/shard_map/ppermute | solution.py:503
  42.9 1.5 %collective-permute-start.7 = (bf16[1024,128]{1,0:T(8,128)(2,1)S(1)}, bf16[1024,128]{1,0:T(8,128)(2,1)S(1)}, u32[]{:S(2)}, u32[]{:S(2)}) collective-permute-start(bf16[1024,128]{1,0:T(8,128)(2,1)S(1)} %collective-permute-done.5.refs_0_), channel_id=1, source_target_pairs={{0,4},{4,8},{8,12},{12,14},{14,10},{10,6},{6,2},{2,0},{1,5},{5,9},... | collective-permute-start | bytes 786440 | tf_op jit(solution)/shard_map/ppermute | solution.py:503
  44.4 5.3 %ring_step.7 = (bf16[49,256,512]{2,1,0:T(8,128)(2,1)S(1)}, f32[9,256,128]{2,1,0:T(8,128)S(1)}, f32[8,128]{1,0:T(8,128)}) custom-call(s32[74]{0:T(128)S(1)} %plan.1.plan_ref, bf16[1024,128]{1,0:T(8,128)(2,1)S(1)} %collective-permute-done.2.refs_0_, bf16[1056,128]{1,0:T(8,128)(2,1)S(1)} %collective-permute-done.12.refs_1_, ...), custom_call_target="tpu_custom_call", output_to_operand_aliasing={{0}: (8, {})} | custom-call | flops 1073741824 | bytes 4194304 | tf_op jit(solution)/shard_map/ring_step/pallas_call | solution.py:325
  49.8 6.7 %ring_step.8 = (bf16[49,256,512]{2,1,0:T(8,128)(2,1)S(1)}, f32[9,256,128]{2,1,0:T(8,128)S(1)}, f32[8,128]{1,0:T(8,128)}) custom-call(s32[74]{0:T(128)S(1)} %plan.1.plan_ref, bf16[1024,128]{1,0:T(8,128)(2,1)S(1)} %collective-permute-done.5.refs_0_, bf16[1056,128]{1,0:T(8,128)(2,1)S(1)} %collective-permute-done.13.refs_1_, ...), custom_call_target="tpu_custom_call", output_to_operand_aliasing={{0}: (8, {})} | custom-call | flops 1073741824 | bytes 4194304 | tf_op jit(solution)/shard_map/ring_step/pallas_call | solution.py:325
  56.5 3.6 %ring_step.9 = (bf16[49,256,512]{2,1,0:T(8,128)(2,1)S(1)}, f32[9,256,128]{2,1,0:T(8,128)S(1)}, f32[8,128]{1,0:T(8,128)}) custom-call(s32[74]{0:T(128)S(1)} %plan.1.plan_ref, bf16[1024,128]{1,0:T(8,128)(2,1)S(1)} %collective-permute-done.7.refs_0_, bf16[1056,128]{1,0:T(8,128)(2,1)S(1)} %collective-permute-done.11.refs_1_, ...), custom_call_target="tpu_custom_call", output_to_operand_aliasing={{0}: (6, {})} | custom-call | flops 1073741824 | bytes 4194304 | tf_op jit(solution)/shard_map/ring_step/pallas_call | solution.py:325
  60.1 1.6 %weighted_products.1 = (bf16[4,4,6,64,128]{4,3,2,1,0:T(8,128)(2,1)S(1)}, f32[4,4,6,64,128]{4,3,2,1,0:T(8,128)S(1)}, bf16[8,128,256]{2,1,0:T(8,128)(2,1)S(1)}, f32[4,128]{1,0:T(4,128)S(1)}, f32[4,128]{1,0:T(4,128)S(1)}) custom-call(s32[74]{0:T(128)S(1)} %plan.1.plan_ref, f32[9,256,128]{2,1,0:T(8,128)S(1)} %get-tuple-element.61.total_ref, ...), custom_call_target="tpu_custom_call" | custom-call | tf_op jit(solution)/shard_map/weighted_products/pallas_call | solution.py:405
  61.8 1.5 %products.1 = (bf16[4,4,6,64,128]{4,3,2,1,0:T(8,128)(2,1)S(1)}, f32[4,4,6,64,128]{4,3,2,1,0:T(8,128)S(1)}) custom-call(s32[74]{0:T(128)S(1)} %plan.1.plan_ref, bf16[8,128,256]{2,1,0:T(8,128)(2,1)S(1)} %get-tuple-element.63.turned_ref, bf16[49,256,512]{2,1,0:T(8,128)(2,1)S(1)} %get-tuple-element.62.states_ref), custom_call_target="tpu_custom_call" | custom-call | tf_op jit(solution)/shard_map/products/pallas_call | solution.py:422
  65.2 1.3 %add_received.2.refs_2_ = bf16[4,8,6,64,128]{4,3,2,1,0:T(8,128)(2,1)} custom-call(f32[4,4,6,64,128]{4,3,2,1,0:T(8,128)S(1)} %get-tuple-element.68.kept_ref, bf16[4,4,6,64,128]{4,3,2,1,0:T(8,128)(2,1)S(1)} %collective-permute-done.17.got_ref), custom_call_target="tpu_custom_call" | custom-call | tf_op jit(solution)/shard_map/add_received/pallas_call | solution.py:456
  67.5 1.9 %add_received.3 = (bf16[4,8,6,64,128]{4,3,2,1,0:T(8,128)(2,1)}, f32[4,128]{1,0:T(4,128)}) custom-call(f32[4,4,6,64,128]{4,3,2,1,0:T(8,128)S(1)} %get-tuple-element.64.kept_ref, bf16[4,4,6,64,128]{4,3,2,1,0:T(8,128)(2,1)S(1)} %collective-permute-done.15.got_ref, f32[4,128]{1,0:T(4,128)S(1)} %get-tuple-element.66.refs_0_, ...), custom_call_target="tpu_custom_call", output_to_operand_aliasing={{0}: (4, {})} | custom-call | tf_op jit(solution)/shard_map/add_received/pallas_call | solution.py:456
  (46 shorter events, 6.8 us)
Async XLA Ops:
  0.6 13.1 %copy-start.1 = (s32[256,1024]{1,0:T(8,128)S(1)}, s32[256,1024]{1,0:T(8,128)}, u32[]{:S(2)}) copy-start(s32[256,1024]{1,0:T(8,128)} %counts_ref.1) | copy-start | bytes 3145732
  0.6 13.1 %copy-start.3 = (f32[1024]{0:T(1024)S(1)}, f32[1024]{0:T(1024)}, u32[]{:S(2)}) copy-start(f32[1024]{0:T(1024)} %param.8) | copy-start | bytes 12292
  2.6 11.3 %copy-start.5 = (s32[64,6]{0,1:T(8,128)S(1)}, s32[64,6]{0,1:T(8,128)}, u32[]{:S(2)}) copy-start(s32[64,6]{0,1:T(8,128)} %param.10) | copy-start | bytes 4612
  2.6 11.4 %copy-start.4 = (s32[64]{0:T(128)S(1)}, s32[64]{0:T(128)}, u32[]{:S(2)}) copy-start(s32[64]{0:T(128)} %fill_ref.1) | copy-start | bytes 772
  2.7 20.6 %copy-start.2 = (bf16[1024,128]{1,0:T(8,128)(2,1)S(1)}, bf16[1024,128]{1,0:T(8,128)(2,1)}, u32[]{:S(2)}) copy-start(bf16[1024,128]{1,0:T(8,128)(2,1)} %first_message.1.refs_0_) | copy-start | bytes 786436
  2.7 11.2 %collective-permute-start = (bf16[1024,128]{1,0:T(8,128)(2,1)}, bf16[1024,128]{1,0:T(8,128)(2,1)S(1)}, u32[]{:S(2)}, u32[]{:S(2)}) collective-permute-start(bf16[1024,128]{1,0:T(8,128)(2,1)} %first_message.1.refs_0_), channel_id=1, source_target_pairs={{0,4},{4,8},{8,12},{12,14},{14,10},{10,6},{6,2},{2,0},{1,5},{5,9},... | collective-permute-start | bytes 786440 | tf_op jit(solution)/shard_map/ppermute | solution.py:503
  5.7 8.2 %collective-permute-start.1 = (bf16[1024,128]{1,0:T(8,128)(2,1)}, bf16[1024,128]{1,0:T(8,128)(2,1)S(1)}, u32[]{:S(2)}, u32[]{:S(2)}) collective-permute-start(bf16[1024,128]{1,0:T(8,128)(2,1)} %first_message.1.refs_0_), channel_id=1, source_target_pairs={{4,0},{8,4},{12,8},{14,12},{10,14},{6,10},{2,6},{0,2},{5,1},{9,5},... | collective-permute-start | bytes 786440 | tf_op jit(solution)/shard_map/ppermute | solution.py:503
  8.2 2.5 %collective-permute-start.3 = (f32[4,1024]{1,0:T(4,128)}, f32[4,1024]{1,0:T(4,128)S(1)}, u32[]{:S(2)}, u32[]{:S(2)}) collective-permute-start(f32[4,1024]{1,0:T(4,128)} %get-tuple-element.38), channel_id=1, source_target_pairs={{0,1},{2,3},{4,5},{6,7},{8,9},{10,11},{12,13},{14,15},{16,17},{18,... | collective-permute-start | bytes 49160 | tf_op jit(solution)/shard_map/ppermute | solution.py:483
  11.3 9.1 %collective-permute-start.6 = (bf16[1056,128]{1,0:T(8,128)(2,1)}, bf16[1056,128]{1,0:T(8,128)(2,1)S(1)}, u32[]{:S(2)}, u32[]{:S(2)}) collective-permute-start(bf16[1056,128]{1,0:T(8,128)(2,1)} %carry_rows.1.refs_1_), channel_id=1, source_target_pairs={{4,0},{8,4},{12,8},{14,12},{10,14},{6,10},{2,6},{0,2},{5,1},{9,5},... | collective-permute-start | bytes 811016 | tf_op jit(solution)/shard_map/ppermute | solution.py:503
  13.2 9.6 %collective-permute-start.4 = (bf16[1056,128]{1,0:T(8,128)(2,1)}, bf16[1056,128]{1,0:T(8,128)(2,1)S(1)}, u32[]{:S(2)}, u32[]{:S(2)}) collective-permute-start(bf16[1056,128]{1,0:T(8,128)(2,1)} %carry_rows.1.refs_1_), channel_id=1, source_target_pairs={{0,4},{4,8},{8,12},{12,14},{14,10},{10,6},{6,2},{2,0},{1,5},{5,9},... | collective-permute-start | bytes 811016 | tf_op jit(solution)/shard_map/ppermute | solution.py:503
  16.5 14.0 %collective-permute-start.2 = (bf16[1024,128]{1,0:T(8,128)(2,1)S(1)}, bf16[1024,128]{1,0:T(8,128)(2,1)S(1)}, u32[]{:S(2)}, u32[]{:S(2)}) collective-permute-start(bf16[1024,128]{1,0:T(8,128)(2,1)S(1)} %collective-permute-done.refs_0_), channel_id=1, source_target_pairs={{0,4},{4,8},{8,12},{12,14},{14,10},{10,6},{6,2},{2,0},{1,5},{5,9},... | collective-permute-start | bytes 786440 | tf_op jit(solution)/shard_map/ppermute | solution.py:503
  18.3 12.2 %collective-permute-start.9 = (bf16[1024,128]{1,0:T(8,128)(2,1)S(1)}, bf16[1024,128]{1,0:T(8,128)(2,1)S(1)}, u32[]{:S(2)}, u32[]{:S(2)}) collective-permute-start(bf16[1024,128]{1,0:T(8,128)(2,1)S(1)} %collective-permute-done.1.refs_2_), channel_id=1, source_target_pairs={{4,0},{8,4},{12,8},{14,12},{10,14},{6,10},{2,6},{0,2},{5,1},{9,5},... | collective-permute-start | bytes 786440 | tf_op jit(solution)/shard_map/ppermute | solution.py:503
  20.4 11.4 %collective-permute-start.8 = (bf16[1056,128]{1,0:T(8,128)(2,1)S(1)}, bf16[1056,128]{1,0:T(8,128)(2,1)S(1)}, u32[]{:S(2)}, u32[]{:S(2)}) collective-permute-start(bf16[1056,128]{1,0:T(8,128)(2,1)S(1)} %collective-permute-done.6.refs_3_), channel_id=1, source_target_pairs={{4,0},{8,4},{12,8},{14,12},{10,14},{6,10},{2,6},{0,2},{5,1},{9,5},... | collective-permute-start | bytes 811016 | tf_op jit(solution)/shard_map/ppermute | solution.py:503
  22.8 12.8 %collective-permute-start.12 = (bf16[1056,128]{1,0:T(8,128)(2,1)S(1)}, bf16[1056,128]{1,0:T(8,128)(2,1)S(1)}, u32[]{:S(2)}, u32[]{:S(2)}) collective-permute-start(bf16[1056,128]{1,0:T(8,128)(2,1)S(1)} %collective-permute-done.4.refs_1_), channel_id=1, source_target_pairs={{0,4},{4,8},{8,12},{12,14},{14,10},{10,6},{6,2},{2,0},{1,5},{5,9},... | collective-permute-start | bytes 811016 | tf_op jit(solution)/shard_map/ppermute | solution.py:503
  23.2 2.8 %copy-start = (bf16[4,8,6,128,128]{4,3,2,1,0:T(8,128)(2,1)S(1)}, bf16[4,8,6,128,128]{4,3,2,1,0:T(8,128)(2,1)}, u32[]{:S(2)}) copy-start(bf16[4,8,6,128,128]{4,3,2,1,0:T(8,128)(2,1)} %refs_4_.3) | copy-start | bytes 18874372
  31.9 9.4 %collective-permute-start.10 = (bf16[1056,128]{1,0:T(8,128)(2,1)S(1)}, bf16[1056,128]{1,0:T(8,128)(2,1)S(1)}, u32[]{:S(2)}, u32[]{:S(2)}) collective-permute-start(bf16[1056,128]{1,0:T(8,128)(2,1)S(1)} %collective-permute-done.8.refs_3_), channel_id=1, source_target_pairs={{4,0},{8,4},{12,8},{14,12},{10,14},{6,10},{2,6},{0,2},{5,1},{9,5},... | collective-permute-start | bytes 811016 | tf_op jit(solution)/shard_map/ppermute | solution.py:503
  33.5 9.4 %collective-permute-start.5 = (bf16[1024,128]{1,0:T(8,128)(2,1)S(1)}, bf16[1024,128]{1,0:T(8,128)(2,1)S(1)}, u32[]{:S(2)}, u32[]{:S(2)}) collective-permute-start(bf16[1024,128]{1,0:T(8,128)(2,1)S(1)} %collective-permute-done.2.refs_0_), channel_id=1, source_target_pairs={{0,4},{4,8},{8,12},{12,14},{14,10},{10,6},{6,2},{2,0},{1,5},{5,9},... | collective-permute-start | bytes 786440 | tf_op jit(solution)/shard_map/ppermute | solution.py:503
  33.9 15.9 %collective-permute-start.14 = (bf16[1024,128]{1,0:T(8,128)(2,1)S(1)}, bf16[1024,128]{1,0:T(8,128)(2,1)S(1)}, u32[]{:S(2)}, u32[]{:S(2)}) collective-permute-start(bf16[1024,128]{1,0:T(8,128)(2,1)S(1)} %collective-permute-done.9.refs_2_), channel_id=1, source_target_pairs={{4,0},{8,4},{12,8},{14,12},{10,14},{6,10},{2,6},{0,2},{5,1},{9,5},... | collective-permute-start | bytes 786440 | tf_op jit(solution)/shard_map/ppermute | solution.py:503
  35.6 14.2 %collective-permute-start.13 = (bf16[1056,128]{1,0:T(8,128)(2,1)S(1)}, bf16[1056,128]{1,0:T(8,128)(2,1)S(1)}, u32[]{:S(2)}, u32[]{:S(2)}) collective-permute-start(bf16[1056,128]{1,0:T(8,128)(2,1)S(1)} %collective-permute-done.12.refs_1_), channel_id=1, source_target_pairs={{0,4},{4,8},{8,12},{12,14},{14,10},{10,6},{6,2},{2,0},{1,5},{5,9},... | collective-permute-start | bytes 811016 | tf_op jit(solution)/shard_map/ppermute | solution.py:503
  41.3 15.2 %collective-permute-start.11 = (bf16[1056,128]{1,0:T(8,128)(2,1)S(1)}, bf16[1056,128]{1,0:T(8,128)(2,1)S(1)}, u32[]{:S(2)}, u32[]{:S(2)}) collective-permute-start(bf16[1056,128]{1,0:T(8,128)(2,1)S(1)} %collective-permute-done.10.refs_3_), channel_id=1, source_target_pairs={{4,0},{8,4},{12,8},{14,12},{10,14},{6,10},{2,6},{0,2},{5,1},{9,5},... | collective-permute-start | bytes 811016 | tf_op jit(solution)/shard_map/ppermute | solution.py:503
  42.9 13.5 %collective-permute-start.7 = (bf16[1024,128]{1,0:T(8,128)(2,1)S(1)}, bf16[1024,128]{1,0:T(8,128)(2,1)S(1)}, u32[]{:S(2)}, u32[]{:S(2)}) collective-permute-start(bf16[1024,128]{1,0:T(8,128)(2,1)S(1)} %collective-permute-done.5.refs_0_), channel_id=1, source_target_pairs={{0,4},{4,8},{8,12},{12,14},{14,10},{10,6},{6,2},{2,0},{1,5},{5,9},... | collective-permute-start | bytes 786440 | tf_op jit(solution)/shard_map/ppermute | solution.py:503
  61.7 3.5 %collective-permute-start.17 = (bf16[4,4,6,64,128]{4,3,2,1,0:T(8,128)(2,1)S(1)}, bf16[4,4,6,64,128]{4,3,2,1,0:T(8,128)(2,1)S(1)}, u32[]{:S(2)}, u32[]{:S(2)}) collective-permute-start(bf16[4,4,6,64,128]{4,3,2,1,0:T(8,128)(2,1)S(1)} %get-tuple-element.69), channel_id=1, source_target_pairs={{0,1},{1,0},{2,3},{3,2},{4,5},{5,4},{6,7},{7,6},{8,9},{9,8},{10,11... | collective-permute-start | bytes 4718600 | tf_op jit(solution)/shard_map/ppermute | solution.py:534
  63.4 4.1 %collective-permute-start.15 = (bf16[4,4,6,64,128]{4,3,2,1,0:T(8,128)(2,1)S(1)}, bf16[4,4,6,64,128]{4,3,2,1,0:T(8,128)(2,1)S(1)}, u32[]{:S(2)}, u32[]{:S(2)}) collective-permute-start(bf16[4,4,6,64,128]{4,3,2,1,0:T(8,128)(2,1)S(1)} %get-tuple-element.65), channel_id=1, source_target_pairs={{0,1},{1,0},{2,3},{3,2},{4,5},{5,4},{6,7},{7,6},{8,9},{9,8},{10,11... | collective-permute-start | bytes 4718600 | tf_op jit(solution)/shard_map/ppermute | solution.py:539
  63.9 3.5 %collective-permute-start.16 = (f32[4,128]{1,0:T(4,128)S(1)}, f32[4,128]{1,0:T(4,128)S(1)}, u32[]{:S(2)}, u32[]{:S(2)}) collective-permute-start(f32[4,128]{1,0:T(4,128)S(1)} %get-tuple-element.67), channel_id=1, source_target_pairs={{0,1},{1,0},{2,3},{3,2},{4,5},{5,4},{6,7},{7,6},{8,9},{9,8},{10,11... | collective-permute-start | bytes 6152 | tf_op jit(solution)/shard_map/ppermute | solution.py:535
where the time goes:
time: 69.7 us; the launch traced here: 69.5 us
  Pallas kernels  39.4 us (57%)
  starting transfers between devices  19.1 us (27%)
  waiting for transfers between devices  6.21 us (9%)
  local copies, waits for them, and re-layouts  3.09 us (4%)
  between operations  1.1 us (2%)
    pallas_call x5, Pallas kernels, take_step(): pl.pallas_call(functools.partial(step_kernel, dims, n, call, groups), in_...  25.5 us
    ppermute x14, starting transfers between devices, send(): return lax.ppermute(message, 'types', way)  17 us
    ppermute x14, waiting for transfers between devices, send(): return lax.ppermute(message, 'types', way)  3.24 us
    pallas_call x2, Pallas kernels, add_received(): pl.pallas_call(functools.partial(add_kernel, dims, group), in_specs=[VMEM...  3.14 us
    unnamed x12, local copies, waits for them, and re-layouts  2.81 us
    pallas_call x1, Pallas kernels, make_plan(): pl.pallas_call(functools.partial(plan_kernel, (brows, slots, width, n, mo...  2.47 us
    pallas_call x1, Pallas kernels, impact_messages(): pl.pallas_call(functools.partial(second_kernel, basis, tile, overall), in...  2.46 us
    pallas_call x1, Pallas kernels, impact_messages(): pl.pallas_call(first_kernel, in_specs=[ANYWHERE, ANYWHERE], out_specs=VME...  1.97 us
  transfers between devices with their start and end apart: 18, of which 5 were waited for; matrix products, arithmetic and copies ran while one was open for 1% of the time, Pallas kernels for 44%

commit v1 on v0

--- a/solution.py
+++ b/solution.py
@@ -506,8 +506,8 @@
     hops = n // 2
     at_up, at_down = [one, two], [one, two]
     for hop in range(1, hops + 1):
-        if 1 < hop < hops:
-            ready = (at_up[0], at_down[0]) + ((plan,) if hop == 2 else ())
+        if hop == 2:
+            ready = (at_up[0], at_down[0], plan)
             at_up = [at_up[0], after(at_up[1], ready)]
             at_down = [at_down[0], after(at_down[1], ready)]
         if hop < hops:

time: 69.7 us -> 71.3 us (1.023)
  Pallas kernels: 39.4 us -> 40.7 us
  starting transfers between devices: 19.1 us -> 20 us
    pallas_call x5, Pallas kernels: 25.5 us -> 26.8 us  [take_step(): pl.pallas_call(functools.partial(step_kernel, dims, n, call, groups), in_...]
    ppermute x14, starting transfers between devices: 17 us -> 17.9 us  [send(): return lax.ppermute(message, 'types', way)]
  transfers between devices with their start and end apart: 18 -> 18, of which waited for: 5 -> 5; matrix products, arithmetic and copies ran while one was open for 1% -> 1% of each run, Pallas kernels for 44% -> 43%
where the time goes in v1:
time: 71.3 us; the launch traced here: 71.7 us
  Pallas kernels  40.7 us (57%)
  starting transfers between devices  20 us (28%)
  waiting for transfers between devices  6.19 us (9%)
  local copies, waits for them, and re-layouts  3.09 us (4%)
  between operations  1.1 us (2%)
    pallas_call x5, Pallas kernels, take_step(): pl.pallas_call(functools.partial(step_kernel, dims, n, call, groups), in_...  26.8 us
    ppermute x14, starting transfers between devices, send(): return lax.ppermute(message, 'types', way)  17.9 us
    ppermute x14, waiting for transfers between devices, send(): return lax.ppermute(message, 'types', way)  3.22 us
    pallas_call x2, Pallas kernels, add_received(): pl.pallas_call(functools.partial(add_kernel, dims, group), in_specs=[VMEM...  3.14 us
    unnamed x12, local copies, waits for them, and re-layouts  2.81 us
    pallas_call x1, Pallas kernels, make_plan(): pl.pallas_call(functools.partial(plan_kernel, (brows, slots, width, n, mo...  2.53 us
    pallas_call x1, Pallas kernels, impact_messages(): pl.pallas_call(functools.partial(second_kernel, basis, tile, overall), in...  2.46 us
    pallas_call x1, Pallas kernels, impact_messages(): pl.pallas_call(first_kernel, in_specs=[ANYWHERE, ANYWHERE], out_specs=VME...  1.97 us
  transfers between devices with their start and end apart: 18, of which 5 were waited for; matrix products, arithmetic and copies ran while one was open for 1% of the time, Pallas kernels for 43%

profile of v1, /device:TPU:0, one launch (start us, length us, event | category | flops | bytes accessed | tf_op | source)
XLA Modules:
  0.0 71.7 jit_solution(2892054766846342300)
XLA Ops:
  0.7 2.0 %first_message.1.refs_0_ = bf16[1024,128]{1,0:T(8,128)(2,1)} custom-call(s32[256,1024]{1,0:T(8,128)} %counts_ref.1, bf16[256,1024]{1,0:T(8,128)(2,1)} %mark_hbm.3), custom_call_target="tpu_custom_call" | custom-call | tf_op jit(solution)/shard_map/first_message/pallas_call | solution.py:102
  2.7 3.1 %collective-permute-start = (bf16[1024,128]{1,0:T(8,128)(2,1)}, bf16[1024,128]{1,0:T(8,128)(2,1)S(1)}, u32[]{:S(2)}, u32[]{:S(2)}) collective-permute-start(bf16[1024,128]{1,0:T(8,128)(2,1)} %first_message.1.refs_0_), channel_id=1, source_target_pairs={{0,4},{4,8},{8,12},{12,14},{14,10},{10,6},{6,2},{2,0},{1,5},{5,9},... | collective-permute-start | bytes 786440 | tf_op jit(solution)/shard_map/ppermute | solution.py:503
  5.8 2.5 %second_message.1 = (bf16[1056,128]{1,0:T(8,128)(2,1)}, f32[4,1024]{1,0:T(4,128)}) custom-call(s32[256,1024]{1,0:T(8,128)} %counts_ref.1, bf16[256,1024]{1,0:T(8,128)(2,1)} %mark_hbm.3), custom_call_target="tpu_custom_call" | custom-call | tf_op jit(solution)/shard_map/second_message/pallas_call | solution.py:115
  8.2 1.5 %collective-permute-start.3 = (f32[4,1024]{1,0:T(4,128)}, f32[4,1024]{1,0:T(4,128)S(1)}, u32[]{:S(2)}, u32[]{:S(2)}) collective-permute-start(f32[4,1024]{1,0:T(4,128)} %get-tuple-element.36), channel_id=1, source_target_pairs={{0,1},{2,3},{4,5},{6,7},{8,9},{10,11},{12,13},{14,15},{16,17},{18,... | collective-permute-start | bytes 49160 | tf_op jit(solution)/shard_map/ppermute | solution.py:483
  11.3 1.8 %collective-permute-start.6 = (bf16[1056,128]{1,0:T(8,128)(2,1)}, bf16[1056,128]{1,0:T(8,128)(2,1)S(1)}, u32[]{:S(2)}, u32[]{:S(2)}) collective-permute-start(bf16[1056,128]{1,0:T(8,128)(2,1)} %carry_rows.1.refs_1_), channel_id=1, source_target_pairs={{4,0},{8,4},{12,8},{14,12},{10,14},{6,10},{2,6},{0,2},{5,1},{9,5},... | collective-permute-start | bytes 811016 | tf_op jit(solution)/shard_map/ppermute | solution.py:503
  14.0 2.5 %plan.1.plan_ref = s32[74]{0:T(128)S(1)} custom-call(s32[64,6]{1,0:T(8,128)S(1)} %copy.14.col_ref, s32[64]{0:T(128)S(1)} %copy-done.4), custom_call_target="tpu_custom_call" | custom-call | tf_op jit(solution)/shard_map/plan/pallas_call | solution.py:217
  16.6 1.9 %collective-permute-start.2 = (bf16[1024,128]{1,0:T(8,128)(2,1)S(1)}, bf16[1024,128]{1,0:T(8,128)(2,1)S(1)}, u32[]{:S(2)}, u32[]{:S(2)}) collective-permute-start(bf16[1024,128]{1,0:T(8,128)(2,1)S(1)} %collective-permute-done.refs_0_), channel_id=1, source_target_pairs={{0,4},{4,8},{8,12},{12,14},{14,10},{10,6},{6,2},{2,0},{1,5},{5,9},... | collective-permute-start | bytes 786440 | tf_op jit(solution)/shard_map/ppermute | solution.py:503
  18.4 2.0 %collective-permute-done.6.refs_3_ = bf16[1056,128]{1,0:T(8,128)(2,1)S(1)} collective-permute-done((bf16[1056,128]{1,0:T(8,128)(2,1)}, bf16[1056,128]{1,0:T(8,128)(2,1)S(1)}, u32[]{:S(2)}, u32[]{:S(2)}) %collective-permute-start.6) | collective-permute-done | bytes 270368 | tf_op jit(solution)/shard_map/ppermute | solution.py:503
  20.4 1.7 %collective-permute-start.8 = (bf16[1056,128]{1,0:T(8,128)(2,1)S(1)}, bf16[1056,128]{1,0:T(8,128)(2,1)S(1)}, u32[]{:S(2)}, u32[]{:S(2)}) collective-permute-start(bf16[1056,128]{1,0:T(8,128)(2,1)S(1)} %collective-permute-done.6.refs_3_), channel_id=1, source_target_pairs={{4,0},{8,4},{12,8},{14,12},{10,14},{6,10},{2,6},{0,2},{5,1},{9,5},... | collective-permute-start | bytes 811016 | tf_op jit(solution)/shard_map/ppermute | solution.py:503
  22.2 1.6 %collective-permute-start.13 = (bf16[1024,128]{1,0:T(8,128)(2,1)S(1)}, bf16[1024,128]{1,0:T(8,128)(2,1)S(1)}, u32[]{:S(2)}, u32[]{:S(2)}) collective-permute-start(bf16[1024,128]{1,0:T(8,128)(2,1)S(1)} %collective-permute-done.1.refs_2_), channel_id=1, source_target_pairs={{4,0},{8,4},{12,8},{14,12},{10,14},{6,10},{2,6},{0,2},{5,1},{9,5},... | collective-permute-start | bytes 786440 | tf_op jit(solution)/shard_map/ppermute | solution.py:503
  24.5 2.8 %copy-done = bf16[4,8,6,128,128]{4,3,2,1,0:T(8,128)(2,1)S(1)} copy-done((bf16[4,8,6,128,128]{4,3,2,1,0:T(8,128)(2,1)S(1)}, bf16[4,8,6,128,128]{4,3,2,1,0:T(8,128)(2,1)}, u32[]{:S(2)}) %copy-start) | copy-done | bytes 6291480
  27.2 4.5 %ring_step.5 = (bf16[49,256,512]{2,1,0:T(8,128)(2,1)S(1)}, f32[9,256,128]{2,1,0:T(8,128)S(1)}, f32[8,128]{1,0:T(8,128)}) custom-call(s32[74]{0:T(128)S(1)} %plan.1.plan_ref, bf16[1024,128]{1,0:T(8,128)(2,1)S(1)} %copy-done.2, bf16[1056,128]{1,0:T(8,128)(2,1)} %carry_rows.1.refs_1_, bf16[4,256,256]{2,1,0:T(8,128)(2,1)S(1)} %select_convert_fusion.refs_2_.refs_4_, ...), custom_call_target="tpu_custom_call" | custom-call | flops 1073741824 | bytes 4194304 | tf_op jit(solution)/shard_map/ring_step/pallas_call | solution.py:325
  32.1 1.8 %collective-permute-start.5 = (bf16[1024,128]{1,0:T(8,128)(2,1)S(1)}, bf16[1024,128]{1,0:T(8,128)(2,1)S(1)}, u32[]{:S(2)}, u32[]{:S(2)}) collective-permute-start(bf16[1024,128]{1,0:T(8,128)(2,1)S(1)} %collective-permute-done.2.refs_0_), channel_id=1, source_target_pairs={{0,4},{4,8},{8,12},{12,14},{14,10},{10,6},{6,2},{2,0},{1,5},{5,9},... | collective-permute-start | bytes 786440 | tf_op jit(solution)/shard_map/ppermute | solution.py:503
  35.0 2.1 %collective-permute-start.14 = (bf16[1024,128]{1,0:T(8,128)(2,1)S(1)}, bf16[1024,128]{1,0:T(8,128)(2,1)S(1)}, u32[]{:S(2)}, u32[]{:S(2)}) collective-permute-start(bf16[1024,128]{1,0:T(8,128)(2,1)S(1)} %collective-permute-done.13.refs_2_), channel_id=1, source_target_pairs={{4,0},{8,4},{12,8},{14,12},{10,14},{6,10},{2,6},{0,2},{5,1},{9,5},... | collective-permute-start | bytes 786440 | tf_op jit(solution)/shard_map/ppermute | solution.py:503
  37.2 5.3 %ring_step.6 = (bf16[49,256,512]{2,1,0:T(8,128)(2,1)S(1)}, f32[9,256,128]{2,1,0:T(8,128)S(1)}, f32[8,128]{1,0:T(8,128)}) custom-call(s32[74]{0:T(128)S(1)} %plan.1.plan_ref, bf16[1024,128]{1,0:T(8,128)(2,1)S(1)} %collective-permute-done.refs_0_, bf16[1056,128]{1,0:T(8,128)(2,1)S(1)} %collective-permute-done.4.refs_1_, ...), custom_call_target="tpu_custom_call", output_to_operand_aliasing={{0}: (8, {})} | custom-call | flops 1073741824 | bytes 4194304 | tf_op jit(solution)/shard_map/ring_step/pallas_call | solution.py:325
  42.6 2.0 %collective-permute-start.10 = (bf16[1056,128]{1,0:T(8,128)(2,1)S(1)}, bf16[1056,128]{1,0:T(8,128)(2,1)S(1)}, u32[]{:S(2)}, u32[]{:S(2)}) collective-permute-start(bf16[1056,128]{1,0:T(8,128)(2,1)S(1)} %collective-permute-done.9.refs_3_), channel_id=1, source_target_pairs={{4,0},{8,4},{12,8},{14,12},{10,14},{6,10},{2,6},{0,2},{5,1},{9,5},... | collective-permute-start | bytes 811016 | tf_op jit(solution)/shard_map/ppermute | solution.py:503
  45.4 6.6 %ring_step.7 = (bf16[49,256,512]{2,1,0:T(8,128)(2,1)S(1)}, f32[9,256,128]{2,1,0:T(8,128)S(1)}, f32[8,128]{1,0:T(8,128)}) custom-call(s32[74]{0:T(128)S(1)} %plan.1.plan_ref, bf16[1024,128]{1,0:T(8,128)(2,1)S(1)} %collective-permute-done.2.refs_0_, bf16[1056,128]{1,0:T(8,128)(2,1)S(1)} %collective-permute-done.11.refs_1_, ...), custom_call_target="tpu_custom_call", output_to_operand_aliasing={{0}: (8, {})} | custom-call | flops 1073741824 | bytes 4194304 | tf_op jit(solution)/shard_map/ring_step/pallas_call | solution.py:325
  52.0 6.0 %ring_step.8 = (bf16[49,256,512]{2,1,0:T(8,128)(2,1)S(1)}, f32[9,256,128]{2,1,0:T(8,128)S(1)}, f32[8,128]{1,0:T(8,128)}) custom-call(s32[74]{0:T(128)S(1)} %plan.1.plan_ref, bf16[1024,128]{1,0:T(8,128)(2,1)S(1)} %collective-permute-done.5.refs_0_, bf16[1056,128]{1,0:T(8,128)(2,1)S(1)} %collective-permute-done.12.refs_1_, ...), custom_call_target="tpu_custom_call", output_to_operand_aliasing={{0}: (8, {})} | custom-call | flops 1073741824 | bytes 4194304 | tf_op jit(solution)/shard_map/ring_step/pallas_call | solution.py:325
  58.1 4.3 %ring_step.9 = (bf16[49,256,512]{2,1,0:T(8,128)(2,1)S(1)}, f32[9,256,128]{2,1,0:T(8,128)S(1)}, f32[8,128]{1,0:T(8,128)}) custom-call(s32[74]{0:T(128)S(1)} %plan.1.plan_ref, bf16[1024,128]{1,0:T(8,128)(2,1)S(1)} %collective-permute-done.7.refs_0_, bf16[1056,128]{1,0:T(8,128)(2,1)S(1)} %collective-permute-done.10.refs_1_, ...), custom_call_target="tpu_custom_call", output_to_operand_aliasing={{0}: (6, {})} | custom-call | flops 1073741824 | bytes 4194304 | tf_op jit(solution)/shard_map/ring_step/pallas_call | solution.py:325
  62.4 1.6 %weighted_products.1 = (bf16[4,4,6,64,128]{4,3,2,1,0:T(8,128)(2,1)S(1)}, f32[4,4,6,64,128]{4,3,2,1,0:T(8,128)S(1)}, bf16[8,128,256]{2,1,0:T(8,128)(2,1)S(1)}, f32[4,128]{1,0:T(4,128)S(1)}, f32[4,128]{1,0:T(4,128)S(1)}) custom-call(s32[74]{0:T(128)S(1)} %plan.1.plan_ref, f32[9,256,128]{2,1,0:T(8,128)S(1)} %get-tuple-element.57.total_ref, ...), custom_call_target="tpu_custom_call" | custom-call | tf_op jit(solution)/shard_map/weighted_products/pallas_call | solution.py:405
  64.1 1.5 %products.1 = (bf16[4,4,6,64,128]{4,3,2,1,0:T(8,128)(2,1)S(1)}, f32[4,4,6,64,128]{4,3,2,1,0:T(8,128)S(1)}) custom-call(s32[74]{0:T(128)S(1)} %plan.1.plan_ref, bf16[8,128,256]{2,1,0:T(8,128)(2,1)S(1)} %get-tuple-element.59.turned_ref, bf16[49,256,512]{2,1,0:T(8,128)(2,1)S(1)} %get-tuple-element.58.states_ref), custom_call_target="tpu_custom_call" | custom-call | tf_op jit(solution)/shard_map/products/pallas_call | solution.py:422
  66.2 1.2 %collective-permute-done.17.got_ref = bf16[4,4,6,64,128]{4,3,2,1,0:T(8,128)(2,1)S(1)} collective-permute-done((bf16[4,4,6,64,128]{4,3,2,1,0:T(8,128)(2,1)S(1)}, bf16[4,4,6,64,128]{4,3,2,1,0:T(8,128)(2,1)S(1)}, u32[]{:S(2)}, u32[]{:S(2)}) %collective-permute-start.17) | collective-permute-done | bytes 1572896 | tf_op jit(solution)/shard_map/ppermute | solution.py:534
  67.5 1.3 %add_received.2.refs_2_ = bf16[4,8,6,64,128]{4,3,2,1,0:T(8,128)(2,1)} custom-call(f32[4,4,6,64,128]{4,3,2,1,0:T(8,128)S(1)} %get-tuple-element.64.kept_ref, bf16[4,4,6,64,128]{4,3,2,1,0:T(8,128)(2,1)S(1)} %collective-permute-done.17.got_ref), custom_call_target="tpu_custom_call" | custom-call | tf_op jit(solution)/shard_map/add_received/pallas_call | solution.py:456
  69.7 1.9 %add_received.3 = (bf16[4,8,6,64,128]{4,3,2,1,0:T(8,128)(2,1)}, f32[4,128]{1,0:T(4,128)}) custom-call(f32[4,4,6,64,128]{4,3,2,1,0:T(8,128)S(1)} %get-tuple-element.60.kept_ref, bf16[4,4,6,64,128]{4,3,2,1,0:T(8,128)(2,1)S(1)} %collective-permute-done.15.got_ref, f32[4,128]{1,0:T(4,128)S(1)} %get-tuple-element.62.refs_0_, ...), custom_call_target="tpu_custom_call", output_to_operand_aliasing={{0}: (4, {})} | custom-call | tf_op jit(solution)/shard_map/add_received/pallas_call | solution.py:456
  (46 shorter events, 7.2 us)
Async XLA Ops:
  0.6 13.1 %copy-start.1 = (s32[256,1024]{1,0:T(8,128)S(1)}, s32[256,1024]{1,0:T(8,128)}, u32[]{:S(2)}) copy-start(s32[256,1024]{1,0:T(8,128)} %counts_ref.1) | copy-start | bytes 3145732
  0.6 13.1 %copy-start.3 = (f32[1024]{0:T(1024)S(1)}, f32[1024]{0:T(1024)}, u32[]{:S(2)}) copy-start(f32[1024]{0:T(1024)} %param.8) | copy-start | bytes 12292
  2.6 11.3 %copy-start.5 = (s32[64,6]{0,1:T(8,128)S(1)}, s32[64,6]{0,1:T(8,128)}, u32[]{:S(2)}) copy-start(s32[64,6]{0,1:T(8,128)} %param.10) | copy-start | bytes 4612
  2.6 11.4 %copy-start.4 = (s32[64]{0:T(128)S(1)}, s32[64]{0:T(128)}, u32[]{:S(2)}) copy-start(s32[64]{0:T(128)} %fill_ref.1) | copy-start | bytes 772
  2.7 21.8 %copy-start.2 = (bf16[1024,128]{1,0:T(8,128)(2,1)S(1)}, bf16[1024,128]{1,0:T(8,128)(2,1)}, u32[]{:S(2)}) copy-start(bf16[1024,128]{1,0:T(8,128)(2,1)} %first_message.1.refs_0_) | copy-start | bytes 786436
  2.7 11.2 %collective-permute-start = (bf16[1024,128]{1,0:T(8,128)(2,1)}, bf16[1024,128]{1,0:T(8,128)(2,1)S(1)}, u32[]{:S(2)}, u32[]{:S(2)}) collective-permute-start(bf16[1024,128]{1,0:T(8,128)(2,1)} %first_message.1.refs_0_), channel_id=1, source_target_pairs={{0,4},{4,8},{8,12},{12,14},{14,10},{10,6},{6,2},{2,0},{1,5},{5,9},... | collective-permute-start | bytes 786440 | tf_op jit(solution)/shard_map/ppermute | solution.py:503
  5.7 8.2 %collective-permute-start.1 = (bf16[1024,128]{1,0:T(8,128)(2,1)}, bf16[1024,128]{1,0:T(8,128)(2,1)S(1)}, u32[]{:S(2)}, u32[]{:S(2)}) collective-permute-start(bf16[1024,128]{1,0:T(8,128)(2,1)} %first_message.1.refs_0_), channel_id=1, source_target_pairs={{4,0},{8,4},{12,8},{14,12},{10,14},{6,10},{2,6},{0,2},{5,1},{9,5},... | collective-permute-start | bytes 786440 | tf_op jit(solution)/shard_map/ppermute | solution.py:503
  8.2 2.5 %collective-permute-start.3 = (f32[4,1024]{1,0:T(4,128)}, f32[4,1024]{1,0:T(4,128)S(1)}, u32[]{:S(2)}, u32[]{:S(2)}) collective-permute-start(f32[4,1024]{1,0:T(4,128)} %get-tuple-element.36), channel_id=1, source_target_pairs={{0,1},{2,3},{4,5},{6,7},{8,9},{10,11},{12,13},{14,15},{16,17},{18,... | collective-permute-start | bytes 49160 | tf_op jit(solution)/shard_map/ppermute | solution.py:483
  11.3 9.1 %collective-permute-start.6 = (bf16[1056,128]{1,0:T(8,128)(2,1)}, bf16[1056,128]{1,0:T(8,128)(2,1)S(1)}, u32[]{:S(2)}, u32[]{:S(2)}) collective-permute-start(bf16[1056,128]{1,0:T(8,128)(2,1)} %carry_rows.1.refs_1_), channel_id=1, source_target_pairs={{4,0},{8,4},{12,8},{14,12},{10,14},{6,10},{2,6},{0,2},{5,1},{9,5},... | collective-permute-start | bytes 811016 | tf_op jit(solution)/shard_map/ppermute | solution.py:503
  13.2 10.6 %collective-permute-start.4 = (bf16[1056,128]{1,0:T(8,128)(2,1)}, bf16[1056,128]{1,0:T(8,128)(2,1)S(1)}, u32[]{:S(2)}, u32[]{:S(2)}) collective-permute-start(bf16[1056,128]{1,0:T(8,128)(2,1)} %carry_rows.1.refs_1_), channel_id=1, source_target_pairs={{0,4},{4,8},{8,12},{12,14},{14,10},{10,6},{6,2},{2,0},{1,5},{5,9},... | collective-permute-start | bytes 811016 | tf_op jit(solution)/shard_map/ppermute | solution.py:503
  16.6 15.5 %collective-permute-start.2 = (bf16[1024,128]{1,0:T(8,128)(2,1)S(1)}, bf16[1024,128]{1,0:T(8,128)(2,1)S(1)}, u32[]{:S(2)}, u32[]{:S(2)}) collective-permute-start(bf16[1024,128]{1,0:T(8,128)(2,1)S(1)} %collective-permute-done.refs_0_), channel_id=1, source_target_pairs={{0,4},{4,8},{8,12},{12,14},{14,10},{10,6},{6,2},{2,0},{1,5},{5,9},... | collective-permute-start | bytes 786440 | tf_op jit(solution)/shard_map/ppermute | solution.py:503
  20.4 11.3 %collective-permute-start.8 = (bf16[1056,128]{1,0:T(8,128)(2,1)S(1)}, bf16[1056,128]{1,0:T(8,128)(2,1)S(1)}, u32[]{:S(2)}, u32[]{:S(2)}) collective-permute-start(bf16[1056,128]{1,0:T(8,128)(2,1)S(1)} %collective-permute-done.6.refs_3_), channel_id=1, source_target_pairs={{4,0},{8,4},{12,8},{14,12},{10,14},{6,10},{2,6},{0,2},{5,1},{9,5},... | collective-permute-start | bytes 811016 | tf_op jit(solution)/shard_map/ppermute | solution.py:503
  22.2 12.8 %collective-permute-start.13 = (bf16[1024,128]{1,0:T(8,128)(2,1)S(1)}, bf16[1024,128]{1,0:T(8,128)(2,1)S(1)}, u32[]{:S(2)}, u32[]{:S(2)}) collective-permute-start(bf16[1024,128]{1,0:T(8,128)(2,1)S(1)} %collective-permute-done.1.refs_2_), channel_id=1, source_target_pairs={{4,0},{8,4},{12,8},{14,12},{10,14},{6,10},{2,6},{0,2},{5,1},{9,5},... | collective-permute-start | bytes 786440 | tf_op jit(solution)/shard_map/ppermute | solution.py:503
  23.8 13.4 %collective-permute-start.11 = (bf16[1056,128]{1,0:T(8,128)(2,1)S(1)}, bf16[1056,128]{1,0:T(8,128)(2,1)S(1)}, u32[]{:S(2)}, u32[]{:S(2)}) collective-permute-start(bf16[1056,128]{1,0:T(8,128)(2,1)S(1)} %collective-permute-done.4.refs_1_), channel_id=1, source_target_pairs={{0,4},{4,8},{8,12},{12,14},{14,10},{10,6},{6,2},{2,0},{1,5},{5,9},... | collective-permute-start | bytes 811016 | tf_op jit(solution)/shard_map/ppermute | solution.py:503
  24.4 2.8 %copy-start = (bf16[4,8,6,128,128]{4,3,2,1,0:T(8,128)(2,1)S(1)}, bf16[4,8,6,128,128]{4,3,2,1,0:T(8,128)(2,1)}, u32[]{:S(2)}) copy-start(bf16[4,8,6,128,128]{4,3,2,1,0:T(8,128)(2,1)} %refs_4_.3) | copy-start | bytes 18874372
  31.8 10.8 %collective-permute-start.9 = (bf16[1056,128]{1,0:T(8,128)(2,1)S(1)}, bf16[1056,128]{1,0:T(8,128)(2,1)S(1)}, u32[]{:S(2)}, u32[]{:S(2)}) collective-permute-start(bf16[1056,128]{1,0:T(8,128)(2,1)S(1)} %collective-permute-done.8.refs_3_), channel_id=1, source_target_pairs={{4,0},{8,4},{12,8},{14,12},{10,14},{6,10},{2,6},{0,2},{5,1},{9,5},... | collective-permute-start | bytes 811016 | tf_op jit(solution)/shard_map/ppermute | solution.py:503
  32.1 12.5 %collective-permute-start.5 = (bf16[1024,128]{1,0:T(8,128)(2,1)S(1)}, bf16[1024,128]{1,0:T(8,128)(2,1)S(1)}, u32[]{:S(2)}, u32[]{:S(2)}) collective-permute-start(bf16[1024,128]{1,0:T(8,128)(2,1)S(1)} %collective-permute-done.2.refs_0_), channel_id=1, source_target_pairs={{0,4},{4,8},{8,12},{12,14},{14,10},{10,6},{6,2},{2,0},{1,5},{5,9},... | collective-permute-start | bytes 786440 | tf_op jit(solution)/shard_map/ppermute | solution.py:503
  35.0 17.0 %collective-permute-start.14 = (bf16[1024,128]{1,0:T(8,128)(2,1)S(1)}, bf16[1024,128]{1,0:T(8,128)(2,1)S(1)}, u32[]{:S(2)}, u32[]{:S(2)}) collective-permute-start(bf16[1024,128]{1,0:T(8,128)(2,1)S(1)} %collective-permute-done.13.refs_2_), channel_id=1, source_target_pairs={{4,0},{8,4},{12,8},{14,12},{10,14},{6,10},{2,6},{0,2},{5,1},{9,5},... | collective-permute-start | bytes 786440 | tf_op jit(solution)/shard_map/ppermute | solution.py:503
  37.2 14.9 %collective-permute-start.12 = (bf16[1056,128]{1,0:T(8,128)(2,1)S(1)}, bf16[1056,128]{1,0:T(8,128)(2,1)S(1)}, u32[]{:S(2)}, u32[]{:S(2)}) collective-permute-start(bf16[1056,128]{1,0:T(8,128)(2,1)S(1)} %collective-permute-done.11.refs_1_), channel_id=1, source_target_pairs={{0,4},{4,8},{8,12},{12,14},{14,10},{10,6},{6,2},{2,0},{1,5},{5,9},... | collective-permute-start | bytes 811016 | tf_op jit(solution)/shard_map/ppermute | solution.py:503
  42.6 15.5 %collective-permute-start.10 = (bf16[1056,128]{1,0:T(8,128)(2,1)S(1)}, bf16[1056,128]{1,0:T(8,128)(2,1)S(1)}, u32[]{:S(2)}, u32[]{:S(2)}) collective-permute-start(bf16[1056,128]{1,0:T(8,128)(2,1)S(1)} %collective-permute-done.9.refs_3_), channel_id=1, source_target_pairs={{4,0},{8,4},{12,8},{14,12},{10,14},{6,10},{2,6},{0,2},{5,1},{9,5},... | collective-permute-start | bytes 811016 | tf_op jit(solution)/shard_map/ppermute | solution.py:503
  44.6 13.5 %collective-permute-start.7 = (bf16[1024,128]{1,0:T(8,128)(2,1)S(1)}, bf16[1024,128]{1,0:T(8,128)(2,1)S(1)}, u32[]{:S(2)}, u32[]{:S(2)}) collective-permute-start(bf16[1024,128]{1,0:T(8,128)(2,1)S(1)} %collective-permute-done.5.refs_0_), channel_id=1, source_target_pairs={{0,4},{4,8},{8,12},{12,14},{14,10},{10,6},{6,2},{2,0},{1,5},{5,9},... | collective-permute-start | bytes 786440 | tf_op jit(solution)/shard_map/ppermute | solution.py:503
  64.0 3.5 %collective-permute-start.17 = (bf16[4,4,6,64,128]{4,3,2,1,0:T(8,128)(2,1)S(1)}, bf16[4,4,6,64,128]{4,3,2,1,0:T(8,128)(2,1)S(1)}, u32[]{:S(2)}, u32[]{:S(2)}) collective-permute-start(bf16[4,4,6,64,128]{4,3,2,1,0:T(8,128)(2,1)S(1)} %get-tuple-element.65), channel_id=1, source_target_pairs={{0,1},{1,0},{2,3},{3,2},{4,5},{5,4},{6,7},{7,6},{8,9},{9,8},{10,11... | collective-permute-start | bytes 4718600 | tf_op jit(solution)/shard_map/ppermute | solution.py:534
  65.6 4.1 %collective-permute-start.15 = (bf16[4,4,6,64,128]{4,3,2,1,0:T(8,128)(2,1)S(1)}, bf16[4,4,6,64,128]{4,3,2,1,0:T(8,128)(2,1)S(1)}, u32[]{:S(2)}, u32[]{:S(2)}) collective-permute-start(bf16[4,4,6,64,128]{4,3,2,1,0:T(8,128)(2,1)S(1)} %get-tuple-element.61), channel_id=1, source_target_pairs={{0,1},{1,0},{2,3},{3,2},{4,5},{5,4},{6,7},{7,6},{8,9},{9,8},{10,11... | collective-permute-start | bytes 4718600 | tf_op jit(solution)/shard_map/ppermute | solution.py:539
  66.2 3.5 %collective-permute-start.16 = (f32[4,128]{1,0:T(4,128)S(1)}, f32[4,128]{1,0:T(4,128)S(1)}, u32[]{:S(2)}, u32[]{:S(2)}) collective-permute-start(f32[4,128]{1,0:T(4,128)S(1)} %get-tuple-element.63), channel_id=1, source_target_pairs={{0,1},{1,0},{2,3},{3,2},{4,5},{5,4},{6,7},{7,6},{8,9},{9,8},{10,11... | collective-permute-start | bytes 6152 | tf_op jit(solution)/shard_map/ppermute | solution.py:535
